TPU v7x, 32 devices: a whole 2x2x4 slice. The times are simulated.
32 devices in a mesh: refl: 4 (over y, core), atom: 8 (over z, x).
Axes of the slice: x: 2, y: 2, z: 4, core: 2. Of those that a mesh axis runs over, the one named last changes fastest.
Arguments:
- features: bfloat16 [16384, 128], P('atom'), may hold values from -6 to 6
- ln_gain: float32 [2, 128], replicated, may hold values from 0.25 to 1.75
- w_qkv: bfloat16 [2, 3, 128, 128], P(None, None, None, 'refl'), may hold values from -0.5 to 0.5
- w_out: bfloat16 [2, 128, 128], replicated, may hold values from -0.5 to 0.5
- w_coord: bfloat16 [3, 128], replicated, may hold values from -0.5 to 0.5
- noisy_coords: float32 [3, 16384], P(None, 'atom'), may hold values from 0 to 1
- scatter_power: float32 [16384], P('atom'), may hold values from 0.5 to 4
- route: int32 [8, 8], P('atom'), may hold values from 0 to 7, each once within a row
- miller: int32 [3, 4096], P(None, 'refl'), may hold values from -12 to 12
- rotations: int32 [4, 3, 3], replicated, may hold values from -1 to 1, as said below
- shifts: float32 [4, 3], replicated, may hold values from 0 to 1
- observed: float32 [4096], P('refl'), may hold values from 0.3 to 3
- obs_weight: float32 [4096], P('refl'), may hold values from 0.2 to 2
Outputs:
- atom_out: bfloat16 [16384, 128], P('atom')
- amplitude: float32 [4096], P(('refl', 'atom'))
- coord_grad: float32 [3, 16384], P(None, 'atom')
Inputs may be any that keep to these rules, and one draw needn't show every extreme that they name: Each row of route names every block of a shard once. `rotations`: each of the 4 matrices is a permutation matrix with signs.
All inputs are finite; a program needn't handle non-finite values.
Results may differ from a plain program's by a relative error of at most 0.012.
Values may be sent and summed in bfloat16 or wider, within the bound.
A program may use at most 64 MiB of HBM per device.

v0:
```python
import math

import jax
import jax.numpy as jnp
from jax import lax
from jax.sharding import PartitionSpec as P

HEAD_FEATURES = 32
QWIN = 32
WINDOW_KEYS = 128
LAYERS = 2


def padded_2(cells, sides, width):
    for axis, dim in sides:
        count = lax.axis_size(axis)
        ends = count - 1
        head = lax.slice_in_dim(cells, 0, width, axis=dim)
        tail = lax.slice_in_dim(cells, cells.shape[dim] - width, cells.shape[dim], axis=dim)
        cells = jnp.concatenate(
            [
                lax.ppermute(tail, axis, [(i, (i + 1) % count) for i in range(ends)]),
                cells,
                lax.ppermute(head, axis, [((i + 1) % count, i) for i in range(ends)]),
            ],
            axis=dim,
        )
    return cells


def layer_norm(x, gain):
    mean = jnp.mean(x, axis=-1, keepdims=True)
    cent = x - mean
    var = jnp.mean(cent * cent, axis=-1, keepdims=True)
    return (cent * lax.rsqrt(var + 1e-05) * gain).astype(jnp.bfloat16)


def window_blocks(padded, window_count):
    parts = [
        padded[QWIN * j : QWIN * j + window_count * QWIN].reshape(window_count, QWIN, -1)
        for j in range(WINDOW_KEYS // QWIN)
    ]
    return jnp.concatenate(parts, axis=1)


def attend_windowed(query_rows, padded_keys, padded_values, valid_mask):
    window_count = query_rows.shape[0] // QWIN
    head_count = query_rows.shape[1] // HEAD_FEATURES
    qwin = query_rows.reshape(window_count, QWIN, head_count, HEAD_FEATURES)
    kwin = window_blocks(padded_keys, window_count).reshape(
        window_count, WINDOW_KEYS, head_count, HEAD_FEATURES
    )
    window_values = window_blocks(padded_values, window_count).reshape(
        window_count, WINDOW_KEYS, head_count, HEAD_FEATURES
    )
    mwin = window_blocks(valid_mask, window_count)[..., 0]
    scores = jnp.einsum(
        "wqhd,wkhd->whqk", qwin, kwin, preferred_element_type=jnp.float32
    ) * HEAD_FEATURES ** (-0.5)
    scores = jnp.where(mwin[:, None, None, :] > 0.5, scores, -1e30)
    top = jnp.max(scores, axis=-1, keepdims=True)
    expo = jnp.exp(scores - top)
    probs = (expo / jnp.sum(expo, axis=-1, keepdims=True)).astype(jnp.bfloat16)
    out = jnp.einsum("whqk,wkhd->wqhd", probs, window_values, preferred_element_type=jnp.float32)
    return out.reshape(window_count * QWIN, head_count * HEAD_FEATURES).astype(jnp.bfloat16)


def phases(hs_blk, tsh_blk, pos):
    turn = (
        hs_blk[:, 0, :, None] * pos[0]
        + hs_blk[:, 1, :, None] * pos[1]
        + hs_blk[:, 2, :, None] * pos[2]
    )
    angle = 2.0 * math.pi * (turn + tsh_blk[:, :, None])
    return (jnp.cos(angle), jnp.sin(angle))


def loss_terms(totals, observed, obs_weight, nrefl):
    amplitude = jnp.sqrt(totals[0] * totals[0] + totals[1] * totals[1] + 1.0)
    slope = 2.0 * obs_weight * (amplitude - observed) / (amplitude * math.sqrt(nrefl))
    return (amplitude, jnp.stack([slope * totals[0], slope * totals[1]]))


def neighbour_rows(keyval, window_border):
    return padded_2(keyval, (("atom", 0),), window_border)


def body(
    features,
    ln_gain,
    w_qkv,
    w_out,
    w_coord,
    noisy_coords,
    scatter_power,
    route,
    miller,
    rotations,
    shifts,
    observed,
    obs_weight,
):
    shards = lax.axis_size("atom")
    rank = lax.axis_index("atom")
    local = features.shape[0]
    natom = local * shards
    window_border = (WINDOW_KEYS - QWIN) // 2
    place = rank * local - window_border + jnp.arange(local + 2 * window_border, dtype=jnp.int32)
    valid_mask = ((place >= 0) & (place < natom)).astype(jnp.float32)[:, None]
    x = features.astype(jnp.float32)
    for layer in range(LAYERS):
        normed = layer_norm(x, ln_gain[layer])
        proj = jnp.einsum(
            "nc,jcd->jnd", normed, w_qkv[layer], preferred_element_type=jnp.float32
        ).astype(jnp.bfloat16)
        width = proj.shape[2]
        keyval = jnp.concatenate([proj[1], proj[2]], axis=1)
        padded = neighbour_rows(keyval, window_border)
        head_rows = attend_windowed(proj[0], padded[:, :width], padded[:, width:], valid_mask)
        out_weight = w_out[layer]
        x = x + jnp.dot(
            lax.all_gather(head_rows, "refl", axis=1, tiled=True),
            out_weight,
            preferred_element_type=jnp.float32,
        )
    atom_out = x.astype(jnp.bfloat16)
    moved = noisy_coords + 0.02 * jnp.dot(w_coord, atom_out.T, preferred_element_type=jnp.float32)
    packed = jnp.concatenate([moved, scatter_power[None, :]], axis=0)
    blk = local // shards
    packed = packed.reshape(4, shards, blk)[:, route[0], :]
    arrived = lax.all_to_all(packed, "atom", split_axis=1, concat_axis=1, tiled=True).reshape(
        4, local
    )
    pos = arrived[:3]
    power = arrived[3]
    group = miller.shape[1]
    nops = rotations.shape[0]
    nrefl = group * lax.axis_size("refl")
    hs = jnp.einsum(
        "skc,kr->scr",
        rotations.astype(jnp.float32),
        miller.astype(jnp.float32),
        precision=lax.Precision.HIGHEST,
    )
    tsh = jnp.einsum(
        "kr,sk->sr", miller.astype(jnp.float32), shifts, precision=lax.Precision.HIGHEST
    )
    norm = 1.0 / math.sqrt(nops * natom)
    rows = min(512, group)
    turns = group // rows
    hs_b = hs.reshape(nops, 3, turns, rows).transpose(2, 0, 1, 3)
    ts_b = tsh.reshape(nops, turns, rows).transpose(1, 0, 2)

    def structure(cosv, sinv):
        fa = jnp.einsum("sra,a->r", cosv, power, precision=lax.Precision.HIGHEST)
        fb = jnp.einsum("sra,a->r", sinv, power, precision=lax.Precision.HIGHEST)
        return jnp.stack([fa, fb]) * norm

    def forward(carry, item):
        cosv, sinv = phases(item[0], item[1], pos)
        return (carry, structure(cosv, sinv))

    unused, parts = lax.scan(forward, 0.0, (hs_b, ts_b))
    partial_sums = parts.transpose(1, 0, 2).reshape(2, group)
    share = group // shards
    totals = lax.psum(partial_sums, "atom")
    amp_all, slopes = loss_terms(totals, observed, obs_weight, nrefl)
    amplitude = lax.dynamic_slice_in_dim(amp_all, rank * share, share, 0)
    sl_b = slopes.reshape(2, turns, rows).transpose(1, 0, 2)
    factor = 2.0 * math.pi * norm

    def accumulate(total, hs_blk, cosv, sinv, slope_blk):
        coef = (
            factor
            * power
            * (cosv * slope_blk[1][None, :, None] - sinv * slope_blk[0][None, :, None])
        )
        return total + jnp.einsum("scr,sra->ca", hs_blk, coef, precision=lax.Precision.HIGHEST)

    empty = jnp.zeros((3, local), jnp.float32)

    def backward(total, item):
        cosv, sinv = phases(item[0], item[1], pos)
        return (accumulate(total, item[0], cosv, sinv, item[2]), None)

    local_grad, unused = lax.scan(backward, empty, (hs_b, ts_b, sl_b))
    coord_grad = lax.psum(local_grad, "refl")
    return (atom_out, amplitude, coord_grad)


def solution(mesh):
    placed = (
        P("atom", None),
        P(),
        P(None, None, None, "refl"),
        P(),
        P(),
        P(None, "atom"),
        P("atom"),
        P("atom", None),
        P(None, "refl"),
        P(),
        P(),
        P("refl"),
        P("refl"),
    )
    return jax.shard_map(
        body,
        mesh=mesh,
        in_specs=placed,
        out_specs=(P("atom", None), P(("refl", "atom")), P(None, "atom")),
        check_vma=False,
    )
```

profile of v0, /device:TPU:0, one launch (start us, length us, event | category | flops | bytes accessed | tf_op | source)
XLA Modules:
  0.0 429.7 jit_solution(12854472690880396493)
XLA Ops:
  0.7 1.3 copy.71
  2.2 0.8 fusion.136
  3.0 0.8 slice_bitcast_fusion.7
  4.3 4.8 %collective-permute-start = (bf16[48,64]{0,1:T(8,128)(2,1)S(1)}, bf16[48,64]{0,1:T(8,128)(2,1)S(1)}, u32[]{:S(2)}, u32[]{:S(2)}) collective-permute-start(bf16[48,64]{0,1:T(8,128)(2,1)S(1)} %get-tuple-element.185), channel_id=1, source_target_pairs={{0,1},{1,2},{2,3},{3,4},{4,5},{5,6},{6,7},{8,9},{9,10},{10,11},{11... | collective-permute-start | bytes 18440 | tf_op jit(solution)/shard_map/ppermute | solution.py:22
  9.1 1.3 collective-permute-start.1
  11.2 3.5 collective-permute-done.1
  15.2 0.4 reshape.317
  15.9 0.4 reshape.318
  16.3 1.1 copy.78
  17.4 0.4 reshape.319
  17.8 1.1 copy.79
  18.9 0.4 reshape.320
  19.3 1.1 copy.80
  20.5 0.4 reshape.312
  20.8 1.2 copy.73
  22.0 0.4 reshape.313
  22.4 1.2 copy.74
  23.5 0.4 reshape.314
  23.9 1.1 copy.75
  25.1 0.4 reshape.315
  25.5 1.1 copy.76
  26.6 3.2 fusion.139
  29.8 2.7 fusion.46
  32.7 0.5 convert_element_type.85
  33.2 7.2 %all_gather.6 = bf16[2048,128]{0,1:T(8,128)(2,1)S(1)} all-gather(bf16[2048,32]{0,1:T(8,128)(2,1)S(1)} %convert_element_type.85), channel_id=1, replica_groups=mesh['refl'=4,'atom'=8] {'refl'}, dimensions={1}, use_global_device_ids=true | all-gather | bytes 655360 | tf_op jit(solution)/shard_map/all_gather | solution.py:122
  41.5 4.3 %collective-permute-start.2 = (bf16[48,64]{0,1:T(8,128)(2,1)S(1)}, bf16[48,64]{0,1:T(8,128)(2,1)S(1)}, u32[]{:S(2)}, u32[]{:S(2)}) collective-permute-start(bf16[48,64]{0,1:T(8,128)(2,1)S(1)} %get-tuple-element.181), channel_id=1, source_target_pairs={{0,1},{1,2},{2,3},{3,4},{4,5},{5,6},{6,7},{8,9},{9,10},{10,11},{11... | collective-permute-start | bytes 18440 | tf_op jit(solution)/shard_map/ppermute | solution.py:22
  45.8 1.5 collective-permute-start.3
  47.6 3.9 collective-permute-done.3
  51.6 0.8 fusion.132
  53.1 0.4 reshape.327
  53.8 0.9 fusion.133
  54.8 1.3 reshape.328
  56.1 1.2 copy.90
  57.2 1.3 reshape.329
  58.5 1.1 copy.91
  59.7 0.4 reshape.321
  60.0 1.1 copy.84
  61.2 1.3 reshape.322
  62.5 1.1 copy.85
  63.6 1.3 reshape.323
  64.9 1.2 copy.86
  66.1 0.4 reshape.324
  66.5 1.1 copy.87
  67.6 3.2 fusion.143
  70.8 2.9 fusion.47
  73.9 0.5 convert_element_type.93
  74.4 6.5 %all_gather.7 = bf16[2048,128]{0,1:T(8,128)(2,1)S(1)} all-gather(bf16[2048,32]{0,1:T(8,128)(2,1)S(1)} %convert_element_type.93), channel_id=1, replica_groups=mesh['refl'=4,'atom'=8] {'refl'}, dimensions={1}, use_global_device_ids=true | all-gather | bytes 655360 | tf_op jit(solution)/shard_map/all_gather | solution.py:122
  81.5 1.2 gather_fusion
  82.7 5.0 %all-to-all-start = ((f32[4,8,256]{2,0,1:T(4,128)}), f32[4,8,256]{2,0,1:T(4,128)S(1)}, u32[]{:S(2)}, u32[]{:S(2)}) async-start(f32[4,8,256]{2,0,1:T(4,128)} %bitcast.47), calls=%async_computation | async-start | bytes 65536 | tf_op jit(solution)/shard_map/all_to_all | solution.py:131
  88.1 1.0 copy.100
  89.1 5.3 %all-to-all-done = f32[4,8,256]{2,0,1:T(4,128)S(1)} async-done(((f32[4,8,256]{2,0,1:T(4,128)}), f32[4,8,256]{2,0,1:T(4,128)S(1)}, u32[]{:S(2)}, u32[]{:S(2)}) %all-to-all-start) | async-done | bytes 32800 | tf_op jit(solution)/shard_map/all_to_all | solution.py:131
  94.4 155.7 %while.21 = (s32[]{:T(128)}, f32[2,2,512]{2,1,0:T(2,128)S(1)}, f32[2,4,3,512]{3,1,2,0:T(4,128)S(1)}, f32[3,2048]{1,0:T(4,128)S(1)}, f32[2,4,512]{2,1,0:T(4,128)S(1)}, /*index=5*/f32[2048]{0:T(1024)S(1)}, s32[]{:T(128)}) while((s32[]{:T(128)}, f32[2,2,512]{2,1,0:T(2,128)S(1)}, f32[2,4,3,512]{3,1,2,0:T(4,128)S(1)}, f32[3,2048]{1,0:T(4,128)S(1)}, ...), condition=%wide.region_11.12_spmd, body=%wide.region_8.11_spmd.sunk | while | flops 60819456 | bytes 33804404 | solution.py:163
  94.5 70.5 %cosine_reduce_fusion.2 = (f32[512,2048]{1,0:T(8,128)}, f32[512,2048]{1,0:T(8,128)S(1)}) fusion(f32[4,512]{1,0:T(4,128)S(1)} %dynamic-slice_bitcast_fusion.8, f32[2048]{0:T(1024)S(1)} %bitcast.254, f32[4,512]{1,0:T(4,128)S(1)} %get-tuple-element.302, f32[2048]{0:T(1024)S(1)} %bitcast.255, f32[4,512]{1,0:T(4,128)S(1)} %get-tuple-element.304, ...), kind=kLoop, calls=%fused_computation.2.clone.1 | loop fusion | flops 35651584 | bytes 8445952 | tf_op jit(solution)/shard_map/while/body/eval_jaxpr/sra,a->r/reduce_sum | solution.py:155
  165.0 3.6 convolution_bitcast_fusion.4
  168.6 3.6 convolution_bitcast_fusion.5
  172.4 70.5 %cosine_reduce_fusion.2 = (f32[512,2048]{1,0:T(8,128)}, f32[512,2048]{1,0:T(8,128)S(1)}) fusion(f32[4,512]{1,0:T(4,128)S(1)} %dynamic-slice_bitcast_fusion.8, f32[2048]{0:T(1024)S(1)} %bitcast.254, f32[4,512]{1,0:T(4,128)S(1)} %get-tuple-element.302, f32[2048]{0:T(1024)S(1)} %bitcast.255, f32[4,512]{1,0:T(4,128)S(1)} %get-tuple-element.304, ...), kind=kLoop, calls=%fused_computation.2.clone.1 | loop fusion | flops 35651584 | bytes 8445952 | tf_op jit(solution)/shard_map/while/body/eval_jaxpr/sra,a->r/reduce_sum | solution.py:155
  242.9 3.6 convolution_bitcast_fusion.4
  246.5 3.6 convolution_bitcast_fusion.5
  250.2 18.3 %psum.14 = f32[2,1024]{1,0:T(2,128)S(1)} all-reduce(f32[2,1024]{1,0:T(2,128)S(1)} %bitcast.266), channel_id=1, replica_groups=mesh['refl'=4,'atom'=8] {'atom'}, use_global_device_ids=true, to_apply=%region_12.13 | all-reduce | flops 2048 | bytes 16384 | tf_op jit(solution)/shard_map/psum | solution.py:166
  268.6 149.2 %while.22 = (s32[]{:T(128)}, f32[3,2048]{1,0:T(4,128)S(1)}, f32[2,4,3,512]{3,2,1,0:T(4,128)S(1)}, f32[2048]{0:T(1024)S(1)}, f32[3,2048]{1,0:T(4,128)S(1)}, /*ind...) while((s32[]{:T(128)}, f32[3,2048]{1,0:T(4,128)S(1)}, ...), condition=%wide.region_14.15_spmd.clone, body=%wide.region_13.14_spmd.clone.sunk | while | flops 197146624 | bytes 381067 | solution.py:186
  268.8 74.4 %fusion.185 = f32[3,2048]{1,0:T(4,128)S(1)} fusion(f32[4,3,512]{2,1,0:T(4,128)S(1)} %dynamic-slice_bitcast_fusion.10, f32[512]{0:T(512)S(1)} %bitcast.260, f32[512]{0:T(512)S(1)} %bitcast.259, f32[4,512]{1,0:T(4,128)S(1)} %dynamic-slice_bitcast_fusion.11, f32[2048]{0:T(1024)S(1)} %bitcast.251, f32[4,512]{1,0:T(4,128)S(1)} %get-tuple-element.321, ...), kind=kOutput, calls=%fused_computation.39.clone.2 | convolution fusion | flops 197144576 | bytes 143361 | tf_op jit(solution)/shard_map/while/body/eval_jaxpr/scr,sra->ca/dot_general | solution.py:178
  343.3 74.4 %fusion.185 = f32[3,2048]{1,0:T(4,128)S(1)} fusion(f32[4,3,512]{2,1,0:T(4,128)S(1)} %dynamic-slice_bitcast_fusion.10, f32[512]{0:T(512)S(1)} %bitcast.260, f32[512]{0:T(512)S(1)} %bitcast.259, f32[4,512]{1,0:T(4,128)S(1)} %dynamic-slice_bitcast_fusion.11, f32[2048]{0:T(1024)S(1)} %bitcast.251, f32[4,512]{1,0:T(4,128)S(1)} %get-tuple-element.321, ...), kind=kOutput, calls=%fused_computation.39.clone.2 | convolution fusion | flops 197144576 | bytes 143361 | tf_op jit(solution)/shard_map/while/body/eval_jaxpr/scr,sra->ca/dot_general | solution.py:178
  417.8 10.9 %psum.15 = f32[3,2048]{1,0:T(4,128)} all-reduce(f32[3,2048]{1,0:T(4,128)S(1)} %get-tuple-element.73), channel_id=1, replica_groups=mesh['refl'=4,'atom'=8] {'refl'}, use_global_device_ids=true, to_apply=%region_15.16 | all-reduce | flops 6144 | bytes 49152 | tf_op jit(solution)/shard_map/psum | solution.py:187
  428.6 0.6 dynamic_slice.21
  (108 shorter events, 6.4 us)
Async XLA Ops:
  0.6 87.1 %copy-start = (f32[4,3]{1,0:T(4,128)S(1)}, f32[4,3]{1,0:T(4,128)}, u32[]{:S(2)}) copy-start(f32[4,3]{1,0:T(4,128)} %param.27) | copy-start | bytes 148
  0.6 9.8 %copy-start.14 = (s32[1,8]{1,0:T(1,128)S(1)}, s32[1,8]{1,0:T(1,128)}, u32[]{:S(2)}) copy-start(s32[1,8]{1,0:T(1,128)} %param.24) | copy-start | bytes 100
  0.7 9.8 %copy-start.10 = (s32[4,3,3]{2,0,1:T(4,128)S(1)}, s32[4,3,3]{2,0,1:T(4,128)}, u32[]{:S(2)}) copy-start(s32[4,3,3]{2,0,1:T(4,128)} %param.26) | copy-start | bytes 436
  0.7 10.0 %copy-start.6 = (s32[3,1024]{1,0:T(4,128)S(1)}, s32[3,1024]{1,0:T(4,128)}, u32[]{:S(2)}) copy-start(s32[3,1024]{1,0:T(4,128)} %param.25) | copy-start | bytes 36868
  4.3 6.9 %collective-permute-start = (bf16[48,64]{0,1:T(8,128)(2,1)S(1)}, bf16[48,64]{0,1:T(8,128)(2,1)S(1)}, u32[]{:S(2)}, u32[]{:S(2)}) collective-permute-start(bf16[48,64]{0,1:T(8,128)(2,1)S(1)} %get-tuple-element.185), channel_id=1, source_target_pairs={{0,1},{1,2},{2,3},{3,4},{4,5},{5,6},{6,7},{8,9},{9,10},{10,11},{11... | collective-permute-start | bytes 18440 | tf_op jit(solution)/shard_map/ppermute | solution.py:22
  9.1 5.6 %collective-permute-start.1 = (bf16[48,64]{0,1:T(8,128)(2,1)S(1)}, bf16[48,64]{0,1:T(8,128)(2,1)S(1)}, u32[]{:S(2)}, u32[]{:S(2)}) collective-permute-start(bf16[48,64]{0,1:T(8,128)(2,1)S(1)} %get-tuple-element.186), channel_id=1, source_target_pairs={{1,0},{2,1},{3,2},{4,3},{5,4},{6,5},{7,6},{9,8},{10,9},{11,10},{12... | collective-permute-start | bytes 18440 | tf_op jit(solution)/shard_map/ppermute | solution.py:24
  19.3 7.3 %copy-start.2 = (bf16[64,32,32]{1,2,0:T(8,128)(2,1)S(1)}, bf16[64,32,32]{1,2,0:T(8,128)(2,1)}, u32[]{:S(2)}) copy-start(bf16[64,32,32]{1,2,0:T(8,128)(2,1)} %copy.78) | copy-start | bytes 393220
  25.4 4.3 %copy-start.3 = (bf16[64,32,32]{1,2,0:T(8,128)(2,1)S(1)}, bf16[64,32,32]{1,2,0:T(8,128)(2,1)}, u32[]{:S(2)}) copy-start(bf16[64,32,32]{1,2,0:T(8,128)(2,1)} %copy.74) | copy-start | bytes 393220
  29.8 10.7 %copy-start.5 = (bf16[2,128,128]{2,1,0:T(8,128)(2,1)S(1)}, bf16[2,128,128]{2,1,0:T(8,128)(2,1)}, u32[]{:S(2)}) copy-start(bf16[2,128,128]{2,1,0:T(8,128)(2,1)} %param.20) | copy-start | bytes 196612
  41.5 6.1 %collective-permute-start.2 = (bf16[48,64]{0,1:T(8,128)(2,1)S(1)}, bf16[48,64]{0,1:T(8,128)(2,1)S(1)}, u32[]{:S(2)}, u32[]{:S(2)}) collective-permute-start(bf16[48,64]{0,1:T(8,128)(2,1)S(1)} %get-tuple-element.181), channel_id=1, source_target_pairs={{0,1},{1,2},{2,3},{3,4},{4,5},{5,6},{6,7},{8,9},{9,10},{10,11},{11... | collective-permute-start | bytes 18440 | tf_op jit(solution)/shard_map/ppermute | solution.py:22
  45.8 5.6 %collective-permute-start.3 = (bf16[48,64]{0,1:T(8,128)(2,1)S(1)}, bf16[48,64]{0,1:T(8,128)(2,1)S(1)}, u32[]{:S(2)}, u32[]{:S(2)}) collective-permute-start(bf16[48,64]{0,1:T(8,128)(2,1)S(1)} %get-tuple-element.182), channel_id=1, source_target_pairs={{1,0},{2,1},{3,2},{4,3},{5,4},{6,5},{7,6},{9,8},{10,9},{11,10},{12... | collective-permute-start | bytes 18440 | tf_op jit(solution)/shard_map/ppermute | solution.py:24
  53.8 5.8 %copy-start.4 = (bf16[2048,32]{0,1:T(8,128)(2,1)S(1)}, bf16[2048,32]{0,1:T(8,128)(2,1)}, u32[]{:S(2)}) copy-start(bf16[2048,32]{0,1:T(8,128)(2,1)} %get-tuple-element.163) | copy-start | bytes 393220
  70.8 10.5 %copy-start.8 = (f32[3,2048]{1,0:T(4,128)S(1)}, f32[3,2048]{1,0:T(4,128)}, u32[]{:S(2)}) copy-start(f32[3,2048]{1,0:T(4,128)} %param.22) | copy-start | bytes 73732
  70.8 10.5 %copy-start.13 = (bf16[3,128]{1,0:T(4,128)(2,1)S(1)}, bf16[3,128]{1,0:T(4,128)(2,1)}, u32[]{:S(2)}) copy-start(bf16[3,128]{1,0:T(4,128)(2,1)} %param.21) | copy-start | bytes 2308
  70.8 10.7 %copy-start.9 = (f32[2048]{0:T(1024)S(1)}, f32[2048]{0:T(1024)}, u32[]{:S(2)}) copy-start(f32[2048]{0:T(1024)} %param.23) | copy-start | bytes 24580
  70.8 17.0 %copy-start.7 = (s32[3,1024]{1,0:T(4,128)S(1)}, s32[3,1024]{1,0:T(4,128)}, u32[]{:S(2)}) copy-start(s32[3,1024]{1,0:T(4,128)} %param.25) | copy-start | bytes 36868
  82.7 11.7 %all-to-all-start = ((f32[4,8,256]{2,0,1:T(4,128)}), f32[4,8,256]{2,0,1:T(4,128)S(1)}, u32[]{:S(2)}, u32[]{:S(2)}) async-start(f32[4,8,256]{2,0,1:T(4,128)} %bitcast.47), calls=%async_computation | async-start | bytes 65536 | tf_op jit(solution)/shard_map/all_to_all | solution.py:131
  94.4 174.1 %copy-start.11 = (f32[1024]{0:T(1024)S(1)}, f32[1024]{0:T(1024)}, u32[]{:S(2)}) copy-start(f32[1024]{0:T(1024)} %param.28) | copy-start | bytes 12292
  94.4 174.1 %copy-start.12 = (f32[1024]{0:T(1024)S(1)}, f32[1024]{0:T(1024)}, u32[]{:S(2)}) copy-start(f32[1024]{0:T(1024)} %param.29) | copy-start | bytes 12292
  165.0 3.6 copy-start.1
  242.9 3.6 copy-start.1
where the time goes:
time: 438 us; the launch traced here: 430 us
  matrix products  177 us (40%)
  other arithmetic  142 us (32%)
  blocking collectives  42.9 us (10%)
  local copies, waits for them, and re-layouts  35.7 us (8%)
  starting transfers between devices  17 us (4%)
  waiting for transfers between devices  12.7 us (3%)
    dot_general x2, matrix products, accumulate(): jnp.einsum('scr,sra->ca', hs_blk, coef, precision=lax.Precision.HIGHEST)  149 us
    reduce_sum x2, other arithmetic, structure(): fa = jnp.einsum('sra,a->r', cosv, power, precision=lax.Precision.HIGHEST)  141 us
    reshape x32, local copies, waits for them, and re-layouts, window_blocks(): padded[QWIN * j:QWIN * j + window_count * QWIN]  25.5 us
    psum x1, blocking collectives, body(): totals = lax.psum(partial_sums, 'atom')  18.3 us
    all_gather x2, blocking collectives, body(): lax.all_gather(head_rows, 'refl', axis=1, tiled=True)  13.7 us
    psum x1, blocking collectives, body(): coord_grad = lax.psum(local_grad, 'refl')  10.9 us
    ppermute x2, starting transfers between devices, padded_2(): lax.ppermute(tail, axis, [(i, (i + 1) % count) for i in range(ends)])  9.17 us
  transfers between devices with their start and end apart: 5, of which 3 were waited for; matrix products, arithmetic and copies ran while one was open for 1% of the time, Pallas kernels for 0%

commit v1 on v0

v1 whole, which is shorter than its diff:
```python
import functools
import math

import jax
import jax.numpy as jnp
from jax import lax
from jax.experimental import pallas as pl
from jax.experimental.pallas import tpu as pltpu
from jax.sharding import PartitionSpec as P

HEAD_FEATURES = 32
QWIN = 32
WINDOW_KEYS = 128
LAYERS = 2
BORDER = (WINDOW_KEYS - QWIN) // 2
HALO = 128
QB = 128
KB = 256
MAXH = 12
KP = 32
LP = MAXH + 1
KL = KP * LP
MESH = pl.DeviceIdType.MESH
VMEM = pl.BlockSpec(memory_space=pltpu.VMEM)
SMEM = pl.BlockSpec(memory_space=pltpu.SMEM)
VLIM = 56 * 1024 * 1024
NT = (((1,), (1,)), ((), ()))


def peers(axis):
    n = lax.axis_size(axis)
    me = lax.axis_index(axis)
    return [lax.rem(me + off, n) for off in range(1, n)]


def greet(ids):
    barrier = pltpu.get_barrier_semaphore()
    for where in ids:
        pl.semaphore_signal(barrier, inc=1, device_id=where, device_id_type=MESH)
    pl.semaphore_wait(barrier, len(ids))


def push(src, dst, send, recv, where):
    return pltpu.make_async_remote_copy(
        src_ref=src, dst_ref=dst, send_sem=send, recv_sem=recv, device_id=where, device_id_type=MESH
    )


def exchange_kernel(axis, shared, src_ref, out_ref, send, recv):
    me = lax.axis_index(axis)
    others = peers(axis)
    greet([{axis: p} for p in others])
    copies = [
        push(src_ref if shared else src_ref.at[p], out_ref.at[me], send.at[i], recv.at[i], {axis: p})
        for i, p in enumerate(others)
    ]
    for c in copies:
        c.start()
    out_ref[me] = src_ref[...] if shared else src_ref[me]
    for c in copies:
        c.wait()


def exchange(src, axis, cid, shared):
    n = lax.axis_size(axis)
    shape = ((n,) + src.shape) if shared else src.shape
    return pl.pallas_call(
        functools.partial(exchange_kernel, axis, shared),
        out_shape=jax.ShapeDtypeStruct(shape, src.dtype),
        in_specs=[VMEM],
        out_specs=VMEM,
        scratch_shapes=[pltpu.SemaphoreType.DMA((n - 1,)), pltpu.SemaphoreType.DMA((n - 1,))],
        compiler_params=pltpu.CompilerParams(collective_id=cid, has_side_effects=True, vmem_limit_bytes=VLIM),
    )(src)


def opening_kernel(w_ref, feat_ref, wg_ref, left_ref, right_ref, send, recv):
    me = lax.axis_index("refl")
    n = lax.axis_size("atom")
    at = lax.axis_index("atom")
    local = feat_ref.shape[0]
    after, before = lax.rem(at + 1, n), lax.rem(at + n - 1, n)
    others = peers("refl")
    greet([{"refl": p} for p in others] + [{"atom": after}, {"atom": before}])
    copies = [
        push(feat_ref.at[pl.ds(local - HALO, HALO)], left_ref, send.at[0], recv.at[0], {"atom": after}),
        push(feat_ref.at[pl.ds(0, HALO)], right_ref, send.at[1], recv.at[1], {"atom": before}),
    ]
    copies += [
        push(w_ref, wg_ref.at[me], send.at[2 + i], recv.at[2 + i], {"refl": p})
        for i, p in enumerate(others)
    ]
    for c in copies:
        c.start()
    wg_ref[me] = w_ref[...]
    for c in copies:
        c.wait()


def opening(wpack, features, cid):
    n = lax.axis_size("refl")
    halo = jax.ShapeDtypeStruct((HALO, features.shape[1]), features.dtype)
    return pl.pallas_call(
        opening_kernel,
        out_shape=(jax.ShapeDtypeStruct((n,) + wpack.shape, wpack.dtype), halo, halo),
        in_specs=[VMEM, VMEM],
        out_specs=(VMEM, VMEM, VMEM),
        scratch_shapes=[pltpu.SemaphoreType.DMA((n + 1,)), pltpu.SemaphoreType.DMA((n + 1,))],
        compiler_params=pltpu.CompilerParams(collective_id=cid, has_side_effects=True, vmem_limit_bytes=VLIM),
    )(wpack, features)


def layer_norm(x, gain):
    mean = jnp.mean(x, axis=-1, keepdims=True)
    cent = x - mean
    var = jnp.mean(cent * cent, axis=-1, keepdims=True)
    return (cent * lax.rsqrt(var + 1e-05) * gain).astype(jnp.bfloat16)


def attention_layer(x_ref, proj_ref, low, high, first_key, natom, band, wg_ref, gain, wout_ref, layer):
    width = x_ref.shape[1]
    per_dev = wg_ref.shape[1] // (LAYERS * width)
    normed = layer_norm(x_ref[low:high, :], gain)
    for dev in range(wg_ref.shape[0]):
        for j in range(per_dev):
            at = (j * LAYERS + layer) * width
            proj_ref[dev * per_dev + j, low:high, :] = jnp.dot(
                normed, wg_ref[dev, at : at + width, :], preferred_element_type=jnp.float32
            ).astype(jnp.bfloat16)
    lane = lax.broadcasted_iota(jnp.int32, (1, KB), 1)
    side = (KB - QB) // 2
    for b in range((high - low - 2 * side) // QB):
        keys = low + b * QB
        place = first_key + keys + lane
        bias = band + jnp.where((place >= 0) & (place < natom), 0.0, -1e30)
        mine = slice(keys + side, keys + side + QB)
        heads = []
        for h in range(proj_ref.shape[0]):
            q = proj_ref[h, mine, 0:HEAD_FEATURES]
            k = proj_ref[h, keys : keys + KB, HEAD_FEATURES : 2 * HEAD_FEATURES]
            v = proj_ref[h, keys : keys + KB, 2 * HEAD_FEATURES : 3 * HEAD_FEATURES]
            scores = lax.dot_general(q, k, NT, preferred_element_type=jnp.float32)
            scores = scores * HEAD_FEATURES ** (-0.5) + bias
            expo = jnp.exp(scores - jnp.max(scores, axis=-1, keepdims=True))
            probs = (expo * (1.0 / jnp.sum(expo, axis=-1, keepdims=True))).astype(jnp.bfloat16)
            o = jnp.dot(probs, v, preferred_element_type=jnp.float32)
            heads.append(o.astype(jnp.bfloat16))
        side_by_side = jnp.concatenate(heads, axis=1)
        x_ref[mine, :] = x_ref[mine, :] + jnp.dot(
            side_by_side, wout_ref[layer], preferred_element_type=jnp.float32
        )


def band_bias():
    a = lax.broadcasted_iota(jnp.int32, (QB, KB), 0)
    c = lax.broadcasted_iota(jnp.int32, (QB, KB), 1)
    rel = c - (KB - QB) // 2 - (a // QWIN) * QWIN
    return jnp.where((rel >= -BORDER) & (rel < WINDOW_KEYS - BORDER), 0.0, -1e30)


def attention_kernel(
    feat_ref, left_ref, right_ref, wg_ref, gain_ref, wout_ref, wc_ref, noisy_ref, power_ref,
    out_ref, packed_ref, ext_ref, x_ref, proj_ref,
):
    local = feat_ref.shape[0]
    sub = out_ref.shape[0]
    rank = lax.axis_index("atom")
    part = lax.axis_index("refl")
    natom = local * lax.axis_size("atom")
    ext_ref[0:HALO] = left_ref[...]
    ext_ref[HALO : HALO + local] = feat_ref[...]
    ext_ref[HALO + local :] = right_ref[...]
    start = pl.multiple_of(part * sub, sub)
    first = rank * local + part * sub - HALO
    band = band_bias()
    rows = sub + 2 * HALO
    x_ref[...] = ext_ref[pl.ds(start, rows), :].astype(jnp.float32)
    side = (KB - QB) // 2
    for layer in range(LAYERS):
        attention_layer(
            x_ref, proj_ref, layer * side, rows - layer * side, first, natom, band,
            wg_ref, gain_ref[layer : layer + 1, :], wout_ref, layer,
        )
    atom_out = x_ref[HALO : HALO + sub, :].astype(jnp.bfloat16)
    out_ref[...] = atom_out
    shift = lax.dot_general(wc_ref[...], atom_out, NT, preferred_element_type=jnp.float32)
    cols = pl.ds(start, sub)
    packed_ref[...] = jnp.zeros_like(packed_ref)
    packed_ref[0:3, :] = noisy_ref[:, cols] + 0.02 * shift[0:3]
    packed_ref[3:4, :] = power_ref[:, cols]


def attention(features, left, right, wg, ln_gain, w_out, w_coord, noisy, power):
    local, width = features.shape
    sub = local // lax.axis_size("refl")
    wc = jnp.pad(w_coord, ((0, 16 - w_coord.shape[0]), (0, 0)))
    return pl.pallas_call(
        attention_kernel,
        out_shape=(
            jax.ShapeDtypeStruct((sub, width), jnp.bfloat16),
            jax.ShapeDtypeStruct((8, sub), jnp.float32),
        ),
        in_specs=[VMEM] * 9,
        out_specs=(VMEM, VMEM),
        scratch_shapes=[
            pltpu.VMEM((local + 2 * HALO, width), jnp.bfloat16),
            pltpu.VMEM((sub + 2 * HALO, width), jnp.float32),
            pltpu.VMEM((wg.shape[0] * wg.shape[1] // (LAYERS * width), sub + 2 * HALO, wg.shape[2]), jnp.bfloat16),
        ],
        compiler_params=pltpu.CompilerParams(vmem_limit_bytes=VLIM),
    )(features, left, right, wg, ln_gain, w_out, wc, noisy, power[None, :])


SIN = [(-1) ** i * math.pi ** (2 * i + 1) / math.factorial(2 * i + 1) for i in range(6)]
COS = [(-1) ** i * math.pi ** (2 * i) / math.factorial(2 * i) for i in range(7)]


def circle(turns):
    r = turns - jnp.floor(turns + 0.5)
    u = r * r
    s = SIN[-1]
    for c in SIN[-2::-1]:
        s = s * u + c
    s = s * r
    c = COS[-1]
    for d in COS[-2::-1]:
        c = c * u + d
    return (1.0 - 2.0 * s * s, 2.0 * s * c)


def tables(pos_ref, cols, width):
    index = lax.broadcasted_iota(jnp.int32, (KP, width), 0).astype(jnp.float32)
    xc, xs = circle((index - MAXH) * pos_ref[0:1, cols])
    yc, ys = circle((index - MAXH) * pos_ref[1:2, cols])
    zc, zs = circle(index[0:16] * pos_ref[2:3, cols])
    return xc, xs, yc, ys, zc, zs


def operator_terms(mil_ref, rot_ref, shift_ref, s):
    mil = [mil_ref[k : k + 1, :] for k in range(3)]
    h = [sum(rot_ref[s * 9 + k * 3 + c] * mil[k] for k in range(3)) for c in range(3)]
    t = sum(mil[k].astype(jnp.float32) * shift_ref[s * 3 + k] for k in range(3))
    tc, ts = circle(t)
    flip = jnp.where(h[2] < 0, -1, 1)
    return (
        h[2] * flip * KP + h[1] * flip + MAXH,
        h[0] * flip + MAXH,
        flip.astype(jnp.float32),
        tc,
        ts,
    )


def hot(index, rows):
    return lax.broadcasted_iota(jnp.int32, (rows, index.shape[1]), 0) == index


def as_bf16(mask):
    return jnp.where(mask, 1.0, 0.0).astype(jnp.bfloat16)


def split2(x):
    hi = x.astype(jnp.bfloat16)
    return hi, (x - hi.astype(jnp.float32)).astype(jnp.bfloat16)


def forward_kernel(chunk, norm, pos_ref, mil_ref, rot_ref, shift_ref, f_ref, xt_ref, yz_ref):
    local = pos_ref.shape[1]
    group = mil_ref.shape[1]
    nops = shift_ref.shape[0] // 3

    def build(i, carry):
        cols = pl.ds(pl.multiple_of(i * chunk, chunk), chunk)
        xc, xs, yc, ys, zc, zs = tables(pos_ref, cols, chunk)
        power = pos_ref[3:4, cols]
        zc, zs = zc * power, zs * power
        xt_ref[0:KP, cols] = xc.astype(jnp.bfloat16)
        xt_ref[KP : 2 * KP, cols] = xs.astype(jnp.bfloat16)
        for l in range(LP):
            a, b = zc[l : l + 1], zs[l : l + 1]
            yz_ref[l * KP : (l + 1) * KP, cols] = (yc * a - ys * b).astype(jnp.bfloat16)
            yz_ref[KL + l * KP : KL + (l + 1) * KP, cols] = (yc * b + ys * a).astype(jnp.bfloat16)
        return carry

    lax.fori_loop(0, local // chunk, build, 0)
    xt = xt_ref[...]
    gc = lax.dot_general(xt, yz_ref[0:KL], NT, preferred_element_type=jnp.float32)
    gs = lax.dot_general(xt, yz_ref[KL:], NT, preferred_element_type=jnp.float32)
    re = gc[0:KP] - gs[KP:]
    im = gs[0:KP] + gc[KP:]
    re_hi, re_lo = split2(re)
    im_hi, im_lo = split2(im)
    grid = jnp.concatenate([re_hi, im_hi, re_lo, im_lo], axis=0)
    fa = jnp.zeros((1, group), jnp.float32)
    fb = jnp.zeros((1, group), jnp.float32)
    for s in range(nops):
        kl, h, flip, tc, ts = operator_terms(mil_ref, rot_ref, shift_ref, s)
        found = jnp.dot(grid, as_bf16(hot(kl, KL)), preferred_element_type=jnp.float32)
        pick = hot(h, KP)
        gre = jnp.sum(jnp.where(pick, found[0:KP] + found[2 * KP : 3 * KP], 0.0), axis=0, keepdims=True)
        gim = flip * jnp.sum(jnp.where(pick, found[KP : 2 * KP] + found[3 * KP :], 0.0), axis=0, keepdims=True)
        fa = fa + tc * gre - ts * gim
        fb = fb + tc * gim + ts * gre
    f_ref[0:1, :] = fa * norm
    f_ref[1:2, :] = fb * norm


def forward(pos, miller, rot, shifts, norm):
    local = pos.shape[1]
    return pl.pallas_call(
        functools.partial(forward_kernel, min(256, local), norm),
        out_shape=jax.ShapeDtypeStruct((2, miller.shape[1]), jnp.float32),
        in_specs=[VMEM, VMEM, SMEM, SMEM],
        out_specs=VMEM,
        scratch_shapes=[
            pltpu.VMEM((2 * KP, local), jnp.bfloat16),
            pltpu.VMEM((2 * KL, local), jnp.bfloat16),
        ],
        compiler_params=pltpu.CompilerParams(vmem_limit_bytes=VLIM),
    )(pos, miller, rot, shifts)


def backward_kernel(
    chunk, factor, nrefl, f_ref, obs_ref, wt_ref, pos_ref, mil_ref, rot_ref, shift_ref,
    amp_ref, grad_ref, w_ref,
):
    local = pos_ref.shape[1]
    nops = shift_ref.shape[0] // 3
    fa = jnp.sum(f_ref[:, 0, :], axis=0, keepdims=True)
    fb = jnp.sum(f_ref[:, 1, :], axis=0, keepdims=True)
    amp = jnp.sqrt(fa * fa + fb * fb + 1.0)
    amp_ref[...] = amp
    slope = 2.0 * wt_ref[...] * (amp - obs_ref[...]) / (amp * math.sqrt(nrefl))
    ga, gb = slope * fa, slope * fb
    total = jnp.zeros((KL, 4 * KP), jnp.float32)
    for s in range(nops):
        kl, h, flip, tc, ts = operator_terms(mil_ref, rot_ref, shift_ref, s)
        vre = tc * ga + ts * gb
        vim = flip * (ts * ga - tc * gb)
        pick = hot(h, KP)
        re_hi, re_lo = split2(jnp.where(pick, vre, 0.0))
        im_hi, im_lo = split2(jnp.where(pick, vim, 0.0))
        spread = jnp.concatenate([re_hi, im_hi, re_lo, im_lo], axis=0)
        total = total + lax.dot_general(as_bf16(hot(kl, KL)), spread, NT, preferred_element_type=jnp.float32)
    wre = total[:, 0:KP] + total[:, 2 * KP : 3 * KP]
    wim = total[:, KP : 2 * KP] + total[:, 3 * KP :]
    hval = (lax.broadcasted_iota(jnp.int32, (1, KP), 1) - MAXH).astype(jnp.float32)
    w_ref[0] = jnp.concatenate([wre, -wim], axis=1).astype(jnp.bfloat16)
    w_ref[1] = jnp.concatenate([wim, wre], axis=1).astype(jnp.bfloat16)
    w_ref[2] = jnp.concatenate([wre * hval, -wim * hval], axis=1).astype(jnp.bfloat16)
    w_ref[3] = jnp.concatenate([wim * hval, wre * hval], axis=1).astype(jnp.bfloat16)
    kval = (lax.broadcasted_iota(jnp.int32, (KP, chunk), 0) - MAXH).astype(jnp.float32)

    def evaluate(i, carry):
        cols = pl.ds(pl.multiple_of(i * chunk, chunk), chunk)
        xc, xs, yc, ys, zc, zs = tables(pos_ref, cols, chunk)
        xt = jnp.concatenate([xc, xs], axis=0).astype(jnp.bfloat16)
        acc = jnp.zeros((KP, chunk), jnp.float32)
        accx, accz = acc, acc
        for l in range(LP):
            rows = pl.ds(l * KP, KP)
            v = [jnp.dot(w_ref[j, rows, :], xt, preferred_element_type=jnp.float32) for j in range(4)]
            a, b = zc[l : l + 1], zs[l : l + 1]
            yzc = yc * a - ys * b
            yzs = yc * b + ys * a
            term = v[1] * yzc + v[0] * yzs
            acc = acc + term
            accx = accx + v[3] * yzc + v[2] * yzs
            accz = accz + float(l) * term
        scale = -factor * pos_ref[3:4, cols]
        grad_ref[0:1, cols] = scale * jnp.sum(accx, axis=0, keepdims=True)
        grad_ref[1:2, cols] = scale * jnp.sum(acc * kval, axis=0, keepdims=True)
        grad_ref[2:3, cols] = scale * jnp.sum(accz, axis=0, keepdims=True)
        return carry

    lax.fori_loop(0, local // chunk, evaluate, 0)


def backward(parts, observed, obs_weight, pos, miller, rot, shifts, factor, nrefl):
    local = pos.shape[1]
    group = miller.shape[1]
    return pl.pallas_call(
        functools.partial(backward_kernel, min(256, local), factor, nrefl),
        out_shape=(
            jax.ShapeDtypeStruct((1, group), jnp.float32),
            jax.ShapeDtypeStruct((3, local), jnp.float32),
        ),
        in_specs=[VMEM] * 5 + [SMEM, SMEM],
        out_specs=(VMEM, VMEM),
        scratch_shapes=[pltpu.VMEM((4, KL, 2 * KP), jnp.bfloat16)],
        compiler_params=pltpu.CompilerParams(vmem_limit_bytes=VLIM),
    )(parts, observed[None, :], obs_weight[None, :], pos, miller, rot, shifts)


def body(
    features,
    ln_gain,
    w_qkv,
    w_out,
    w_coord,
    noisy_coords,
    scatter_power,
    route,
    miller,
    rotations,
    shifts,
    observed,
    obs_weight,
):
    shards = lax.axis_size("atom")
    groups = lax.axis_size("refl")
    rank = lax.axis_index("atom")
    local, width = features.shape
    natom = local * shards
    group = miller.shape[1]
    nops = rotations.shape[0]
    nrefl = group * groups
    norm = 1.0 / math.sqrt(nops * natom)

    per_dev = w_qkv.shape[3] // HEAD_FEATURES
    wpack = w_qkv.reshape(LAYERS, 3, width, per_dev, HEAD_FEATURES).transpose(3, 0, 2, 1, 4)
    wpack = wpack.reshape(per_dev * LAYERS * width, 3 * HEAD_FEATURES)
    wpack = jnp.pad(wpack, ((0, 0), (0, 128 - 3 * HEAD_FEATURES)))
    wg, left, right = opening(wpack, features, 0)
    own_out, own_packed = attention(
        features, left, right, wg, ln_gain, w_out, w_coord, noisy_coords, scatter_power
    )
    atom_out = lax.all_gather(own_out, "refl", axis=0, tiled=True)
    packed = exchange(own_packed, "refl", 1, True).transpose(1, 0, 2).reshape(8, local)

    rot = rotations.reshape(-1)
    sh = shifts.reshape(-1)
    own_f = forward(packed, miller, rot, sh, norm)

    blk = local // shards
    routed = packed[:4].reshape(4, shards, blk)[:, route[0], :].transpose(1, 0, 2)
    routed = routed.reshape(shards, 4 * blk // 128, 128)
    mine = jnp.broadcast_to(own_f.reshape(1, 2 * group // 128, 128), (shards, 2 * group // 128, 128))
    came = exchange(jnp.concatenate([mine, routed], axis=1), "atom", 2, False)
    f_parts = came[:, : 2 * group // 128].reshape(shards, 2, group)
    pos = came[:, 2 * group // 128 :].reshape(shards, 4, blk).transpose(1, 0, 2).reshape(4, local)

    amp, grad = backward(
        f_parts, observed, obs_weight, pos, miller, rot, sh, 2.0 * math.pi * norm, nrefl
    )
    share = group // shards
    amplitude = lax.dynamic_slice_in_dim(amp[0], rank * share, share, 0)
    grads = exchange(grad.reshape(3 * local // 128, 128), "refl", 3, True)
    coord_grad = jnp.sum(grads, axis=0).reshape(3, local)
    return (atom_out, amplitude, coord_grad)


def solution(mesh):
    placed = (
        P("atom", None),
        P(),
        P(None, None, None, "refl"),
        P(),
        P(),
        P(None, "atom"),
        P("atom"),
        P("atom", None),
        P(None, "refl"),
        P(),
        P(),
        P("refl"),
        P("refl"),
    )
    return jax.shard_map(
        body,
        mesh=mesh,
        in_specs=placed,
        out_specs=(P("atom", None), P(("refl", "atom")), P(None, "atom")),
        check_vma=False,
    )
```

time: 438 us -> 79.3 us (0.18); the launches traced: 430 us -> 78.4 us
  matrix products: 177 us -> 0 us
  other arithmetic: 142 us -> 1.57 us
  Pallas kernels: 0 us -> 53.9 us
  blocking collectives: 42.9 us -> 7.66 us
  local copies, waits for them, and re-layouts: 35.7 us -> 14.5 us
  starting transfers between devices: 17 us -> 0 us
  waiting for transfers between devices: 12.7 us -> 0 us
    dot_general x13 -> x0, matrix products: 170 us -> none  [the longest x2 149 us: accumulate(): jnp.einsum('scr,sra->ca', hs_blk, coef, precision=lax.Precision.HIGHEST)]
    reduce_sum x5 -> x1, other arithmetic: 141 us -> 0.91 us  [body(): coord_grad = jnp.sum(grads, axis=0).reshape(3, local)]
    pallas_call x0 -> x7, Pallas kernels: none -> 53.9 us  [the longest x3 18.5 us: exchange(): pl.pallas_call(functools.partial(exchange_kernel, axis, shared), out_shap...]
    psum x2 -> x0, blocking collectives: 29.2 us -> none  [the longest x1 18.3 us: body(): totals = lax.psum(partial_sums, 'atom')]
    reshape x35 -> x9, local copies, waits for them, and re-layouts: 25.6 us -> 4.05 us  [the longest x1 1.38 us: body(): grads = exchange(grad.reshape(3 * local // 128, 128), 'refl', 3, True)]
    ppermute x4 -> x0, starting transfers between devices: 11.9 us -> none  [the longest x2 9.17 us: padded_2(): lax.ppermute(tail, axis, [(i, (i + 1) % count) for i in range(ends)])]
    ppermute x4 -> x0, waiting for transfers between devices: 7.39 us -> none  [the longest x2 7.39 us: padded_2(): lax.ppermute(head, axis, [((i + 1) % count, i) for i in range(ends)])]
    sub x2 -> x0, matrix products: 6.34 us -> none  [attend_windowed(): expo = jnp.exp(scores - top)]
  transfers between devices with their start and end apart: 5 -> 0, of which waited for: 3 -> 0; matrix products, arithmetic and copies ran while one was open for 1% -> 0% of each run, Pallas kernels for 0% -> 0%
where the time goes in v1:
time: 79.3 us; the launch traced here: 78.4 us
  Pallas kernels  53.9 us (68%)
  local copies, waits for them, and re-layouts  14.5 us (18%)
  blocking collectives  7.66 us (10%)
  other arithmetic  1.57 us (2%)
    pallas_call x3, Pallas kernels, exchange(): pl.pallas_call(functools.partial(exchange_kernel, axis, shared), out_shap...  18.5 us
    pallas_call x1, Pallas kernels, opening(): pl.pallas_call(opening_kernel, out_shape=(jax.ShapeDtypeStruct((n,) + wpa...  11.9 us
    pallas_call x1, Pallas kernels, attention(): pl.pallas_call(attention_kernel, out_shape=(jax.ShapeDtypeStruct((sub, wi...  11.9 us
    all_gather x1, blocking collectives, body(): atom_out = lax.all_gather(own_out, 'refl', axis=0, tiled=True)  7.66 us
    pallas_call x1, Pallas kernels, backward(): pl.pallas_call(functools.partial(backward_kernel, min(256, local), factor...  6.36 us
    pallas_call x1, Pallas kernels, forward(): pl.pallas_call(functools.partial(forward_kernel, min(256, local), norm),...  5.34 us
    unnamed x12, local copies, waits for them, and re-layouts  3.51 us

profile of v1, /device:TPU:0, one launch (start us, length us, event | category | flops | bytes accessed | tf_op | source)
XLA Modules:
  0.0 78.4 jit_solution(17929340518713127748)
XLA Ops:
  0.6 0.8 %copy.19 = bf16[1,2,128,3,32]{2,1,4,3,0:T(2,128)(2,1)S(1)} copy(bf16[1,2,128,3,32]{2,4,3,1,0:T(8,128)(2,1)} %bitcast.35) | data formatting | bytes 98304 | tf_op jit(solution)/shard_map/transpose | solution.py:421
  1.5 0.1 copy.20
  1.6 0.7 pad.8.w_ref
  2.3 11.9 %shard_map.148 = (bf16[4,256,128]{2,1,0:T(8,128)(2,1)}, bf16[128,128]{1,0:T(8,128)(2,1)}, bf16[128,128]{1,0:T(8,128)(2,1)}) custom-call(bf16[256,128]{1,0:T(8,128)(2,1)} %pad.8.w_ref, bf16[2048,128]{1,0:T(8,128)(2,1)} %feat_ref.3), custom_call_target="tpu_custom_call" | custom-call | tf_op jit(solution)/shard_map/pallas_call | solution.py:103
  14.2 0.0 copy-start.2
  14.2 0.7 copy-done.2
  14.8 0.6 pad.9.wc_ref
  15.4 11.9 %shard_map.149 = (bf16[512,128]{1,0:T(8,128)(2,1)}, f32[8,512]{1,0:T(8,128)}) custom-call(bf16[2048,128]{1,0:T(8,128)(2,1)} %feat_ref.3, bf16[128,128]{1,0:T(8,128)(2,1)} %get-tuple-element.10.left_ref, bf16[128,128]{1,0:T(8,128)(2,1)} %get-tuple-element.11.right_ref, bf16[4,256,128]{2,1,0:T(8,128)(2,1)} %get-tuple-element.12.wg_ref, f32[2,128]{1,0:T(2,128)} %gain_ref.1, ...), custom_call_target="tpu_custom_call" | custom-call | tf_op jit(solution)/shard_map/pallas_call | solution.py:197
  27.3 7.7 %all_gather.3 = bf16[2048,128]{1,0:T(8,128)(2,1)S(1)} all-gather(bf16[512,128]{1,0:T(8,128)(2,1)} %get-tuple-element.13), channel_id=1, replica_groups=mesh['refl'=4,'atom'=8] {'refl'}, dimensions={0}, use_global_device_ids=true | all-gather | bytes 655360 | tf_op jit(solution)/shard_map/all_gather | solution.py:428
  35.0 5.2 %shard_map.150 = f32[4,8,512]{2,1,0:T(8,128)} custom-call(f32[8,512]{1,0:T(8,128)} %get-tuple-element.14.src_ref), custom_call_target="tpu_custom_call" | custom-call | tf_op jit(solution)/shard_map/pallas_call | solution.py:67
  40.1 0.8 %slice.15 = f32[4,4,512]{2,0,1:T(4,128)S(1)} slice(f32[8,4,512]{2,0,1:T(8,128)} %bitcast.28), slice={[0:4], [0:4], [0:512]} | slice | bytes 65536 | tf_op jit(solution)/shard_map/slice | solution.py:436
  41.0 0.0 copy-start.3
  41.0 0.7 copy-done.3
  41.6 0.6 gather_fusion
  42.2 0.0 copy-start
  42.2 0.7 copy-done
  42.9 0.0 copy-start.1
  42.9 0.6 reshape.78.rot_ref
  43.5 0.1 copy-done.1
  43.6 0.6 reshape.79.shift_ref
  44.2 5.3 %shard_map.151 = f32[2,1024]{1,0:T(2,128)} custom-call(f32[8,2048]{1,0:T(8,128)} %bitcast.29, s32[3,1024]{1,0:T(4,128)} %mil_ref.3, s32[36]{0:T(128)} %reshape.78.rot_ref, f32[12]{0:T(128)} %reshape.79.shift_ref), custom_call_target="tpu_custom_call" | custom-call | tf_op jit(solution)/shard_map/pallas_call | solution.py:310
  49.6 0.7 broadcast_in_dim.18
  50.3 0.7 pad_maximum_fusion.src_ref
  50.9 8.1 %shard_map.152 = f32[8,24,128]{2,1,0:T(8,128)} custom-call(f32[8,24,128]{2,1,0:T(8,128)} %pad_maximum_fusion.src_ref), custom_call_target="tpu_custom_call" | custom-call | tf_op jit(solution)/shard_map/pallas_call | solution.py:67
  59.0 0.0 slice-start
  59.0 0.8 %slice-done = f32[8,16,128]{2,1,0:T(8,128)S(1)} async-done(((f32[8,24,128]{2,1,0:T(8,128)}), f32[8,16,128]{2,1,0:T(8,128)S(1)}, s32[]{:S(2)}) %slice-start) | async-done | bytes 65560 | tf_op jit(solution)/shard_map/slice | solution.py:440
  59.8 0.7 reshape.82.f_ref
  60.5 0.0 slice-start.1
  60.5 0.8 slice-done.1
  61.3 0.6 copy.26
  61.9 6.4 %shard_map.153 = (f32[1,1024]{1,0:T(1,128)}, f32[3,2048]{1,0:T(4,128)}) custom-call(f32[8,2,1024]{2,1,0:T(2,128)} %reshape.82.f_ref, f32[1,1024]{1,0:T(1,128)} %bitcast.37, f32[1,1024]{1,0:T(1,128)} %bitcast.38, f32[4,2048]{1,0:T(4,128)} %bitcast.34, s32[3,1024]{1,0:T(4,128)} %mil_ref.3, s32[36]{0:T(128)} %reshape.78.rot_ref, f32[12]{0:T(128)} %reshape.79.shift_ref), custom_call_target="tpu_custom_call" | custom-call | tf_op jit(solution)/shard_map/pallas_call | solution.py:382
  68.3 1.1 %dynamic-slice_bitcast_fusion = f32[128]{0:T(128)} fusion(f32[1,1024]{1,0:T(1,128)} %get-tuple-element.15, s32[]{:T(128)S(6)} %select_n.14), kind=kLoop, calls=%fused_computation.7 | loop fusion | bytes 1028 | tf_op jit(solution)/shard_map/dynamic_slice | solution.py:447
  69.4 1.4 %reshape.85.src_ref = f32[48,128]{1,0:T(8,128)} reshape(f32[3,2048]{1,0:T(4,128)} %get-tuple-element.16) | data formatting | bytes 49152 | tf_op jit(solution)/shard_map/reshape | solution.py:448
  70.8 5.3 %shard_map.154 = f32[4,48,128]{2,1,0:T(8,128)} custom-call(f32[48,128]{1,0:T(8,128)} %reshape.85.src_ref), custom_call_target="tpu_custom_call" | custom-call | tf_op jit(solution)/shard_map/pallas_call | solution.py:67
  76.1 0.9 %reduce_sum.9 = f32[48,128]{1,0:T(8,128)S(1)} reduce(f32[4,48,128]{2,1,0:T(8,128)} %shard_map.154, f32[]{:T(128)} %constant.17.clone.1), dimensions={0}, to_apply=%region_0.1 | reduce | flops 18432 | bytes 122884 | tf_op jit(solution)/shard_map/reduce_sum | solution.py:449
  77.0 0.6 reshape.86
  77.6 0.8 %copy.32 = bf16[2048,128]{1,0:T(8,128)(2,1)} copy(bf16[2048,128]{1,0:T(8,128)(2,1)S(1)} %all_gather.3) | data formatting | bytes 1048576
  (8 shorter events, 0.1 us)
Async XLA Ops:
  14.2 0.7 copy-start.2
  41.0 0.7 copy-start.3
  42.2 0.7 copy-start
  42.9 0.7 copy-start.1
  59.0 0.8 %slice-start = ((f32[8,24,128]{2,1,0:T(8,128)}), f32[8,16,128]{2,1,0:T(8,128)S(1)}, s32[]{:S(2)}) async-start(f32[8,24,128]{2,1,0:T(8,128)} %shard_map.152), calls=%async_computation | async-start | bytes 131072 | tf_op jit(solution)/shard_map/slice | solution.py:440
  60.5 0.8 slice-start.1
